TPU v7x, 32 devices: a whole 2x2x4 slice. The times are simulated.
32 devices in a mesh: tm: 16 (over z, x, core), head: 2 (over y).
Axes of the slice: x: 2, y: 2, z: 4, core: 2. Of those that a mesh axis runs over, the one named last changes fastest.
Arguments:
- frames: bfloat16 [32768, 1024], P('tm'), may hold values from -6 to 6
- conv_weight: bfloat16 [4, 1024], replicated, may hold values from -3 to 3
- w_query: bfloat16 [1024, 1024], P(None, 'head'), may hold values from -0.1875 to 0.1875
- w_key: bfloat16 [1024, 1024], P(None, 'head'), may hold values from -0.1875 to 0.1875
- w_value: bfloat16 [1024, 1024], P(None, 'head'), may hold values from -0.1875 to 0.1875
- w_gate: bfloat16 [1024, 1024], P(None, 'head'), may hold values from -0.1875 to 0.1875
- w_out: bfloat16 [1024, 1024], P('head'), may hold values from -0.1875 to 0.1875
- norm_gain: float32 [1024], P('head'), may hold values from 0.1 to 1.9
Outputs:
- layer_out: bfloat16 [32768, 1024], P('tm', 'head')
All inputs are finite; a program needn't handle non-finite values.
Results may differ from a plain program's by a relative error of at most 0.014.
Values may be sent and summed in bfloat16 or wider, within the bound.
A program may use at most 64 MiB of HBM per device.

v0:
```python
import jax
import jax.numpy as jnp
from jax import lax
from jax.sharding import PartitionSpec as P

HEAD_DIM = 128
CONV = 4
BLOCK = 512


def from_behind(array, axis, by):
    devices = lax.axis_size(axis)
    pairs = [(i, i + by) for i in range(devices) if 0 <= i + by < devices]
    return lax.ppermute(array, axis, pairs)


def feature_map(inputs):
    return jnp.where(inputs > 0, inputs + 1.0, jnp.exp(jnp.minimum(inputs, 0.0)))


def on_device(frames, conv_weight, w_query, w_key, w_value, w_gate, w_out, norm_gain):
    tok_rows = frames.shape[0]
    edge_rows = from_behind(frames[tok_rows - (CONV - 1) :], "tm", 1)
    padded = jnp.concatenate([edge_rows, frames], axis=0)
    taps = conv_weight.astype(jnp.float32)
    mixed = taps[0] * padded[0:tok_rows].astype(jnp.float32)
    for offset in range(1, CONV):
        mixed = mixed + taps[offset] * padded[offset : offset + tok_rows].astype(jnp.float32)
    smooth = mixed.astype(jnp.bfloat16)
    queries = feature_map(jnp.dot(smooth, w_query, preferred_element_type=jnp.float32)).astype(
        jnp.bfloat16
    )
    key_feats = feature_map(jnp.dot(smooth, w_key, preferred_element_type=jnp.float32)).astype(
        jnp.bfloat16
    )
    values = jnp.dot(smooth, w_value, preferred_element_type=jnp.float32).astype(jnp.bfloat16)
    gates = jnp.dot(smooth, w_gate, preferred_element_type=jnp.float32)
    heads_here = w_query.shape[1] // HEAD_DIM
    blocks = tok_rows // BLOCK
    block_shape = (blocks, BLOCK, heads_here, HEAD_DIM)
    query_blocks = queries.reshape(block_shape)
    key_blocks = key_feats.reshape(block_shape)
    value_blocks = values.reshape(block_shape)
    block_states = jnp.einsum(
        "bthd,bthe->bhde", key_blocks, value_blocks, preferred_element_type=jnp.float32
    )
    own_total = jnp.sum(block_states, axis=0)
    position = lax.axis_index("tm")
    shard_piece = lax.all_gather(own_total[None], "tm", axis=0, tiled=True)
    source_rank = jnp.arange(shard_piece.shape[0], dtype=jnp.int32)
    earlier_mask = (source_rank < position).astype(jnp.float32)
    incoming = jnp.sum(shard_piece * earlier_mask[:, None, None, None], axis=0)
    running_sums = jnp.cumsum(block_states, axis=0)
    exclusive = jnp.concatenate([jnp.zeros_like(block_states[:1]), running_sums[:-1]], axis=0)
    carried = (incoming[None] + exclusive).astype(jnp.bfloat16)
    causal = jnp.tril(jnp.ones((BLOCK, BLOCK), jnp.bool_))
    scores = jnp.einsum(
        "bthd,bshd->bhts", query_blocks, key_blocks, preferred_element_type=jnp.float32
    )
    scores = jnp.where(causal[None, None], scores, 0.0).astype(jnp.bfloat16)
    attended = jnp.einsum(
        "bhts,bshd->bthd", scores, value_blocks, preferred_element_type=jnp.float32
    )
    attended = attended + jnp.einsum(
        "bthd,bhde->bthe", query_blocks, carried, preferred_element_type=jnp.float32
    )
    attended = attended.reshape(tok_rows, heads_here, HEAD_DIM)
    mean_square = jnp.mean(attended * attended, axis=-1, keepdims=True)
    normed = attended * lax.rsqrt(mean_square + 1e-06) * norm_gain.reshape(heads_here, HEAD_DIM)
    normed = normed * jax.nn.silu(gates).reshape(tok_rows, heads_here, HEAD_DIM)
    gated = normed.reshape(tok_rows, heads_here * HEAD_DIM).astype(jnp.bfloat16)
    partial_value = jnp.dot(gated, w_out, preferred_element_type=jnp.float32)
    summed = lax.psum_scatter(
        partial_value.astype(jnp.bfloat16), "head", scatter_dimension=1, tiled=True
    )
    return summed


def solution(mesh):
    placed = (
        P("tm", None),
        P(),
        P(None, "head"),
        P(None, "head"),
        P(None, "head"),
        P(None, "head"),
        P("head", None),
        P("head"),
    )
    return jax.shard_map(
        on_device, mesh=mesh, in_specs=placed, out_specs=P("tm", "head"), check_vma=False
    )
```

profile of v0, /device:TPU:0, one launch (start us, length us, event | category | flops | bytes accessed | tf_op | source)
XLA Modules:
  0.0 189.0 jit_solution(16404768144078657780)
XLA Ops:
  6.5 0.8 slice.28
  7.4 2.3 %collective-permute-start = (bf16[3,1024]{1,0:T(4,128)(2,1)S(1)}, bf16[3,1024]{1,0:T(4,128)(2,1)S(1)}, u32[]{:S(2)}, u32[]{:S(2)}) collective-permute-start(bf16[3,1024]{1,0:T(4,128)(2,1)S(1)} %slice.28), channel_id=1, source_target_pairs={{0,2},{2,4},{4,6},{6,8},{8,10},{10,12},{12,14},{14,16},{16,18},{18... | collective-permute-start | bytes 18440 | tf_op jit(solution)/shard_map/ppermute | solution.py:14
  9.7 0.9 fusion.17
  10.6 11.6 %add_convert_fusion = bf16[2048,1024]{1,0:T(8,128)(2,1)S(1)} fusion(bf16[2048,1024]{1,0:T(8,128)(2,1)} %param.8, bf16[3,1024]{1,0:T(4,128)(2,1)S(1)} %collective-permute-done, f32[1024]{0:T(1024)S(1)} %bitcast.42, f32[1024]{0:T(1024)S(1)} %bitcast.41, f32[1024]{0:T(1024)S(1)} %bitcast.40, f32[1024]{0:T(1024)S(1)} %bitcast.39), kind=kLoop, calls=%fused_computation.1 | loop fusion | flops 44040192 | bytes 8411136 | tf_op jit(solution)/shard_map/convert_element_type | solution.py:29
  22.2 1.9 %copy-done.2 = bf16[2048,1024]{1,0:T(8,128)(2,1)} copy-done((bf16[2048,1024]{1,0:T(8,128)(2,1)}, bf16[2048,1024]{1,0:T(8,128)(2,1)S(1)}, u32[]{:S(2)}) %copy-start.2) | copy-done | bytes 4194328
  24.2 2.9 %select_convert_fusion.1 = bf16[2048,512]{1,0:T(8,128)(2,1)S(1)} fusion(bf16[2048,1024]{1,0:T(8,128)(2,1)S(1)} %add_convert_fusion, bf16[1024,512]{1,0:T(8,128)(2,1)S(1)} %copy-done.4), kind=kOutput, calls=%fused_computation.14 | convolution fusion | flops 2152726528 | bytes 7340032 | tf_op jit(solution)/shard_map/dot_general | solution.py:33
  27.1 2.0 %reshape.51 = bf16[4,512,4,128]{3,2,1,0:T(4,128)(2,1)} reshape(bf16[2048,512]{1,0:T(8,128)(2,1)S(1)} %select_convert_fusion.1) | data formatting | bytes 4194304 | tf_op jit(solution)/shard_map/reshape | solution.py:42
  29.1 3.0 %copy.24 = bf16[4,512,4,128]{1,3,2,0:T(8,128)(2,1)S(1)} copy(bf16[4,512,4,128]{3,2,1,0:T(4,128)(2,1)} %reshape.51) | data formatting | bytes 4194304 | tf_op jit(solution)/shard_map/reshape | solution.py:42
  32.1 6.2 %convolution_convert_fusion.1 = bf16[2048,512]{1,0:T(8,128)(2,1)} fusion(bf16[2048,1024]{1,0:T(8,128)(2,1)} %copy-done.2, bf16[1024,512]{1,0:T(8,128)(2,1)} %param.12), kind=kOutput, calls=%fused_computation.17 | convolution fusion | flops 2148532224 | bytes 7340032 | tf_op jit(solution)/shard_map/dot_general | solution.py:36
  38.2 4.0 %reshape.49 = bf16[4,512,4,128]{3,2,1,0:T(4,128)(2,1)} reshape(bf16[2048,512]{1,0:T(8,128)(2,1)} %convolution_convert_fusion.1) | data formatting | bytes 4194304 | tf_op jit(solution)/shard_map/reshape | solution.py:43
  42.2 4.1 %fusion.18 = (f32[4,128,128]{2,1,0:T(8,128)}, f32[4,4,128,128]{3,2,1,0:T(8,128)}) fusion(bf16[4,512,4,128]{1,3,2,0:T(8,128)(2,1)S(1)} %copy.24, bf16[4,512,4,128]{3,2,1,0:T(4,128)(2,1)} %reshape.49), kind=kOutput, calls=%fused_computation.33 | convolution fusion | flops 268632064 | bytes 5505024 | tf_op jit(solution)/shard_map/bthd,bthe->bhde/dot_general | solution.py:44
  46.4 6.7 %select_convert_fusion.2 = bf16[2048,512]{1,0:T(8,128)(2,1)} fusion(bf16[2048,1024]{1,0:T(8,128)(2,1)} %copy-done.2, bf16[1024,512]{1,0:T(8,128)(2,1)} %param.10), kind=kOutput, calls=%fused_computation.15 | convolution fusion | flops 2152726528 | bytes 7340032 | tf_op jit(solution)/shard_map/dot_general | solution.py:30
  53.1 4.0 %reshape.50 = bf16[4,512,4,128]{3,2,1,0:T(4,128)(2,1)} reshape(bf16[2048,512]{1,0:T(8,128)(2,1)} %select_convert_fusion.2) | data formatting | bytes 4194304 | tf_op jit(solution)/shard_map/reshape | solution.py:41
  57.1 1.3 fusion.21
  58.5 0.9 slice.44
  59.4 9.2 %fusion.5 = f32[4,4,128,512]{3,2,1,0:T(8,128)} fusion(bf16[4,512,4,128]{1,3,2,0:T(8,128)(2,1)S(1)} %copy.24, pred[512,512]{1,0:T(8,128)(4,1)S(1)} %iota_compare_fusion, bf16[4,512,4,128]{3,2,1,0:T(4,128)(2,1)} %reshape.49, bf16[4,512,4,128]{3,2,1,0:T(4,128)(2,1)} %reshape.50), kind=kOutput, calls=%fused_computation.18 | convolution fusion | flops 2155872256 | bytes 10747904 | tf_op jit(solution)/shard_map/bhts,bshd->bthd/dot_general | solution.py:61
  68.6 32.9 %all-gather.3.cloned.1.call-done = f32[64,128,128]{2,1,0:T(8,128)} async-done(((f32[4,128,128]{2,1,0:T(8,128)}), f32[64,128,128]{2,1,0:T(8,128)}) %all-gather.3.cloned.1.call-update) | async-done | bytes 4194320 | tf_op jit(solution)/shard_map/all_gather | solution.py:49
  101.6 2.7 %multiply_reduce_fusion.1 = f32[4,128,128]{2,1,0:T(8,128)S(1)} fusion(f32[16,4,128,128]{3,2,1,0:T(8,128)} %bitcast.36, f32[16]{0:T(128)S(1)} %compare_convert_fusion), kind=kLoop, calls=%fused_computation.13 | loop fusion | flops 2031616 | bytes 4456512 | tf_op jit(solution)/shard_map/reduce_sum | solution.py:52
  104.3 5.1 %multiply_reduce_fusion = (f32[4,512,4]{1,2,0:T(4,128)S(1)}, f32[4,512,4,128]{1,3,2,0:T(8,128)}) fusion(f32[4,4,128,512]{3,2,1,0:T(8,128)} %fusion.5, bf16[4,512,4,128]{3,2,1,0:T(4,128)(2,1)S(1)} %copy-done.1, f32[3,4,128,128]{3,2,1,0:T(8,128)S(1)} %copy-done.3, f32[4,128,128]{2,1,0:T(8,128)S(1)} %multiply_reduce_fusion.1), kind=kOutput, calls=%fused_computation.11 | convolution fusion | flops 272097280 | bytes 11567104 | tf_op jit(solution)/shard_map/bthd,bhde->bthe/dot_general | solution.py:64
  109.4 0.4 copy.29
  109.8 5.2 %copy.28 = f32[4,512,4,128]{3,2,1,0:T(4,128)} copy(f32[4,512,4,128]{1,3,2,0:T(8,128)} %get-tuple-element.12) | data formatting | bytes 8388608 | tf_op jit(solution)/shard_map/add | solution.py:64
  115.0 3.8 %mul.95 = f32[2048,4,128]{2,1,0:T(4,128)} broadcast(f32[2048,4]{1,0:T(8,128)S(1)} %copy.29), dimensions={0,1} | broadcast | bytes 4227072 | tf_op jit(solution)/shard_map/mul | solution.py:69
  118.9 10.3 %convolution_convert_fusion = bf16[2048,1024]{1,0:T(8,128)(2,1)} fusion(bf16[512,1024]{1,0:T(8,128)(2,1)S(1)} %copy-done, f32[256,8,4,128]{3,2,1,0:T(4,128)} %bitcast.35, f32[256,8,4,128]{3,2,1,0:T(4,128)} %bitcast.37, f32[512]{0:T(512)S(1)} %copy-done.6, bf16[2048,1024]{1,0:T(8,128)(2,1)} %copy-done.2, bf16[1024,512]{1,0:T(8,128)(2,1)S(1)} %copy-done.5), kind=kOutput, calls=%fused_computation.16 | convolution fusion | flops 4305453056 | bytes 18876416 | tf_op jit(solution)/shard_map/dot_general | solution.py:72
  129.2 53.0 %reduce-scatter.2.cloned.1.call-done = bf16[2048,512]{1,0:T(8,128)(2,1)} async-done(((bf16[2048,1024]{1,0:T(8,128)(2,1)}), bf16[2048,512]{1,0:T(8,128)(2,1)}) %reduce-scatter.2.cloned.1.call-update) | async-done | bytes 2097168 | tf_op jit(solution)/shard_map/reduce_scatter | solution.py:73
  (21 shorter events, 0.2 us)
Async XLA Ops:
  6.5 112.4 %copy-start = (bf16[512,1024]{1,0:T(8,128)(2,1)S(1)}, bf16[512,1024]{1,0:T(8,128)(2,1)}, u32[]{:S(2)}) copy-start(bf16[512,1024]{1,0:T(8,128)(2,1)} %param.14) | copy-start | bytes 3145732
  6.5 95.0 %all-gather.3.cloned.1.call-start = ((), (), s32[]{:S(2)}) async-start(), calls=%async_computation.2 | async-start | bytes 4456448 | tf_op jit(solution)/shard_map/all_gather | solution.py:49
  7.4 3.2 %collective-permute-start = (bf16[3,1024]{1,0:T(4,128)(2,1)S(1)}, bf16[3,1024]{1,0:T(4,128)(2,1)S(1)}, u32[]{:S(2)}, u32[]{:S(2)}) collective-permute-start(bf16[3,1024]{1,0:T(4,128)(2,1)S(1)} %slice.28), channel_id=1, source_target_pairs={{0,2},{2,4},{4,6},{6,8},{8,10},{10,12},{12,14},{14,16},{16,18},{18... | collective-permute-start | bytes 18440 | tf_op jit(solution)/shard_map/ppermute | solution.py:14
  10.6 13.6 %copy-start.4 = (bf16[1024,512]{1,0:T(8,128)(2,1)S(1)}, bf16[1024,512]{1,0:T(8,128)(2,1)}, u32[]{:S(2)}) copy-start(bf16[1024,512]{1,0:T(8,128)(2,1)} %param.11) | copy-start | bytes 3145732
  22.2 1.9 %copy-start.2 = (bf16[2048,1024]{1,0:T(8,128)(2,1)}, bf16[2048,1024]{1,0:T(8,128)(2,1)S(1)}, u32[]{:S(2)}) copy-start(bf16[2048,1024]{1,0:T(8,128)(2,1)S(1)} %add_convert_fusion) | copy-start | bytes 12582916
  46.3 135.9 %reduce-scatter.2.cloned.1.call-start = ((), (), s32[]{:S(2)}) async-start(), calls=%async_computation.1 | async-start | bytes 6291456 | tf_op jit(solution)/shard_map/reduce_scatter | solution.py:73
  68.6 35.6 %copy-start.1 = (bf16[4,512,4,128]{3,2,1,0:T(4,128)(2,1)S(1)}, bf16[4,512,4,128]{3,2,1,0:T(4,128)(2,1)}, u32[]{:S(2)}) copy-start(bf16[4,512,4,128]{3,2,1,0:T(4,128)(2,1)} %reshape.50) | copy-start | bytes 6291460
  101.6 2.7 %copy-start.3 = (f32[3,4,128,128]{3,2,1,0:T(8,128)S(1)}, f32[3,4,128,128]{3,2,1,0:T(8,128)}, u32[]{:S(2)}) copy-start(f32[3,4,128,128]{3,2,1,0:T(8,128)} %slice.44) | copy-start | bytes 2359300
  115.0 3.8 %copy-start.5 = (bf16[1024,512]{1,0:T(8,128)(2,1)S(1)}, bf16[1024,512]{1,0:T(8,128)(2,1)}, u32[]{:S(2)}) copy-start(bf16[1024,512]{1,0:T(8,128)(2,1)} %param.13) | copy-start | bytes 3145732
  115.0 3.8 %copy-start.6 = (f32[512]{0:T(512)S(1)}, f32[512]{0:T(512)}, u32[]{:S(2)}) copy-start(f32[512]{0:T(512)} %param.15) | copy-start | bytes 6148
Sparse Core Ops, SparseCore 0:
  46.4 55.1 all-gather.2
  129.3 52.7 reduce-scatter.1
where the time goes:
time: 190 us; the launch traced here: 189 us
  waiting for transfers between devices  85.9 us (45%)
  matrix products  44.4 us (23%)
  local copies, waits for them, and re-layouts  27 us (14%)
  other arithmetic  15.8 us (8%)
  between operations  13.5 us (7%)
  starting transfers between devices  2.39 us (1%)
    reduce_scatter x1, waiting for transfers between devices, on_device(): lax.psum_scatter(partial_value.astype(jnp.bfloat16), 'head', scatter_dime...  53 us
    all_gather x1, waiting for transfers between devices, on_device(): shard_piece = lax.all_gather(own_total[None], 'tm', axis=0, tiled=True)  32.9 us
    convert_element_type x1, other arithmetic, on_device(): smooth = mixed.astype(jnp.bfloat16)  11.6 us
    dot_general x1, matrix products, on_device(): partial_value = jnp.dot(gated, w_out, preferred_element_type=jnp.float32)  10.3 us
    dot_general x1, matrix products, on_device(): jnp.einsum('bhts,bshd->bthd', scores, value_blocks, preferred_element_typ...  9.22 us
    dot_general x1, matrix products, on_device(): jnp.dot(smooth, w_query, preferred_element_type=jnp.float32)  6.7 us
    dot_general x1, matrix products, on_device(): jnp.dot(smooth, w_value, preferred_element_type=jnp.float32)  6.15 us
    add x1, local copies, waits for them, and re-layouts, on_device(): attended + jnp.einsum('bthd,bhde->bthe', query_blocks, carried, preferred...  5.24 us
  transfers between devices with their start and end apart: 3, of which 2 were waited for; matrix products, arithmetic and copies ran while one was open for 12% of the time, Pallas kernels for 0%

commit v1 on v0

--- a/solution.py
+++ b/solution.py
@@ -1,6 +1,10 @@
+import functools
+
 import jax
 import jax.numpy as jnp
 from jax import lax
+from jax.experimental import pallas as pl
+from jax.experimental.pallas import tpu as pltpu
 from jax.sharding import PartitionSpec as P
 
 HEAD_DIM = 128
@@ -18,7 +22,7 @@
     return jnp.where(inputs > 0, inputs + 1.0, jnp.exp(jnp.minimum(inputs, 0.0)))
 
 
-def on_device(frames, conv_weight, w_query, w_key, w_value, w_gate, w_out, norm_gain):
+def on_device_collectives(frames, conv_weight, w_query, w_key, w_value, w_gate, w_out, norm_gain):
     tok_rows = frames.shape[0]
     edge_rows = from_behind(frames[tok_rows - (CONV - 1) :], "tm", 1)
     padded = jnp.concatenate([edge_rows, frames], axis=0)
@@ -76,6 +80,300 @@
     return summed
 
 
+F32 = jnp.float32
+BF16 = jnp.bfloat16
+MESH = pl.DeviceIdType.MESH
+N_COPIES = 29
+
+
+def fused_kernel(
+    n_tm, frames, conv, wq, wk, wv, wg, wo, gain, out,
+    smooth, qs, ks, vs, gs, wx, wox, gainx, halo, ext, state, carried,
+    total, pair, before, incoming,
+    s_tot, r_tot, s_pair, r_pair, s_grp, r_grp, s_bef, r_bef, s_inc, r_inc,
+    send_sem, recv_sem,
+):
+    t = lax.axis_index("tm")
+    h = lax.axis_index("head")
+    rows = frames.shape[0]
+    half = wq.shape[1]
+    heads = half // HEAD_DIM
+    blocks = rows // BLOCK
+    depth = wq.shape[0]
+    quarter = depth // 4
+    quarter_o = half // 4
+    n_z = n_tm // 4
+    z = lax.div(t, 4)
+    r = lax.rem(t, 4)
+    x = lax.div(r, 2)
+    c = lax.rem(t, 2)
+    other_core = {"tm": t + 1 - 2 * c}
+    other_x = {"tm": t + 2 - 4 * x}
+    other_y = {"head": 1 - h}
+    after = {"tm": lax.rem(t + 1, n_tm)}
+    ahead = {"tm": lax.rem(t + n_tm - 1, n_tm)}
+    zs = [{"tm": lax.rem(z + d, n_z) * 4 + r} for d in range(1, n_z)]
+    r_x = r + 2 - 4 * x
+
+    barrier = pltpu.get_barrier_semaphore()
+    peers = [other_core, other_x, other_y, after, ahead] + zs
+    for peer in peers:
+        pl.semaphore_signal(barrier, inc=1, device_id=peer, device_id_type=MESH)
+    pl.semaphore_wait(barrier, len(peers))
+
+    copies = []
+
+    def send(src, dst, device):
+        n = len(copies)
+        copy = pltpu.make_async_remote_copy(
+            src_ref=src, dst_ref=dst, send_sem=send_sem.at[n], recv_sem=recv_sem.at[n],
+            device_id=device, device_id_type=MESH,
+        )
+        copy.start()
+        copies.append(copy)
+        return copy
+
+    def piece(m, which):
+        if m == 4:
+            return wox.at[pl.ds(pl.multiple_of(which * quarter_o, quarter_o), quarter_o), :]
+        return wx.at[m, pl.ds(pl.multiple_of(which * quarter, quarter), quarter), :]
+
+    edge = send(frames.at[pl.ds(rows - 16, 16), :], halo, after)
+    from_y, from_x, from_core = {}, {}, {}
+    for m, weight in enumerate((wk, wv, wq, wg)):
+        mine = weight.at[pl.ds(pl.multiple_of(r * quarter, quarter), quarter), :]
+        from_y[m] = send(mine, piece(m, r), other_y)
+    mine = wo.at[
+        pl.ds(pl.multiple_of(r * quarter_o, quarter_o), quarter_o),
+        pl.ds(pl.multiple_of((1 - h) * half, half), half),
+    ]
+    from_y[4] = send(mine, piece(4, r), other_y)
+    gain_copy = send(gain, gainx, other_y)
+
+    def relay_y(m):
+        from_y[m].wait_recv()
+        from_x[m] = send(piece(m, r), piece(m, r), other_x)
+        from_core[m] = [send(piece(m, r), piece(m, r), other_core)]
+
+    def relay_x(m):
+        from_x[m].wait_recv()
+        from_core[m].append(send(piece(m, r_x), piece(m, r_x), other_core))
+
+    def ready(m):
+        for copy in from_core[m]:
+            copy.wait_recv()
+
+    chunk = BLOCK // 2
+    taps = conv[...].astype(F32)
+
+    def mix(first):
+        ext[16 : 16 + chunk, :] = frames[pl.ds(first, chunk), :].astype(F32)
+        mixed = taps[0:1] * ext[13 : 13 + chunk, :]
+        for j in range(1, CONV):
+            mixed = mixed + taps[j : j + 1] * ext[13 + j : 13 + j + chunk, :]
+        smooth[pl.ds(first, chunk), :] = mixed.astype(BF16)
+
+    def mix_chunk(i, _):
+        first = pl.multiple_of(i * chunk, chunk)
+        ext[0:16, :] = frames[pl.ds(pl.multiple_of(first - 16, 16), 16), :].astype(F32)
+        mix(first)
+        return 0
+
+    lax.fori_loop(1, rows // chunk, mix_chunk, 0)
+    edge.wait_recv()
+    ext[0:16, :] = halo[...].astype(F32) * jnp.minimum(t, 1).astype(F32)
+    mix(0)
+
+    def project(weight, into, which, function):
+        def step(i, _):
+            at = pl.ds(pl.multiple_of(i * BLOCK, BLOCK), BLOCK)
+            product = jnp.dot(smooth[at, :], weight[...], preferred_element_type=F32)
+            into[which, at, :] = function(product).astype(BF16)
+            return 0
+
+        lax.fori_loop(0, blocks, step, 0)
+
+    def silu_by(gain_ref):
+        def function(v):
+            return (0.5 * v) * (1.0 + jnp.tanh(0.5 * v)) * gain_ref[...]
+
+        return function
+
+    def same(v):
+        return v
+
+    def states(which):
+        def step(b, _):
+            at = pl.ds(pl.multiple_of(b * BLOCK, BLOCK), BLOCK)
+            for j in range(heads):
+                cols = slice(j * HEAD_DIM, (j + 1) * HEAD_DIM)
+                state[which, b, cols, :] = lax.dot_general(
+                    ks[which, at, cols], vs[which, at, cols],
+                    (((0,), (0,)), ((), ())), preferred_element_type=F32,
+                )
+            return 0
+
+        lax.fori_loop(0, blocks, step, 0)
+
+    def carry(which, start_ref):
+        running = start_ref[...].astype(F32)
+        for b in range(blocks):
+            carried[which, b] = running.astype(BF16)
+            if b + 1 < blocks:
+                running = running + state[which, b]
+
+    row_id = lax.broadcasted_iota(jnp.int32, (chunk, chunk), 0)
+    col_id = lax.broadcasted_iota(jnp.int32, (chunk, chunk), 1)
+    causal = col_id <= row_id
+    nt = (((1,), (1,)), ((), ()))
+
+    def attend(which):
+        def step(b, _):
+            low = pl.ds(pl.multiple_of(b * BLOCK, BLOCK), chunk)
+            high = pl.ds(pl.multiple_of(b * BLOCK + chunk, chunk), chunk)
+            for j in range(heads):
+                cols = slice(j * HEAD_DIM, (j + 1) * HEAD_DIM)
+                q0, q1 = qs[which, low, cols], qs[which, high, cols]
+                k0, k1 = ks[which, low, cols], ks[which, high, cols]
+                v0, v1 = vs[which, low, cols], vs[which, high, cols]
+                start = carried[which, b, cols, :]
+                s00 = lax.dot_general(q0, k0, nt, preferred_element_type=F32)
+                s10 = lax.dot_general(q1, k0, nt, preferred_element_type=F32)
+                s11 = lax.dot_general(q1, k1, nt, preferred_element_type=F32)
+                s00 = jnp.where(causal, s00, 0.0).astype(BF16)
+                s11 = jnp.where(causal, s11, 0.0).astype(BF16)
+                a0 = jnp.dot(s00, v0, preferred_element_type=F32)
+                a0 = a0 + jnp.dot(q0, start, preferred_element_type=F32)
+                a1 = jnp.dot(s10.astype(BF16), v0, preferred_element_type=F32)
+                a1 = a1 + jnp.dot(s11, v1, preferred_element_type=F32)
+                a1 = a1 + jnp.dot(q1, start, preferred_element_type=F32)
+                for at, a in ((low, a0), (high, a1)):
+                    scale = lax.rsqrt(jnp.mean(a * a, axis=-1, keepdims=True) + 1e-06)
+                    gated = a * scale * gs[which, at, cols].astype(F32)
+                    qs[which, at, cols] = gated.astype(BF16)
+            return 0
+
+        lax.fori_loop(0, blocks, step, 0)
+
+    here = pl.ds(pl.multiple_of(c * (half // 2), half // 2), half // 2)
+    there = pl.ds(pl.multiple_of((1 - c) * (half // 2), half // 2), half // 2)
+
+    project(wk, ks, 0, feature_map)
+    relay_y(0)
+    project(wv, vs, 0, same)
+    states(0)
+    sums = state[0, 0]
+    for b in range(1, blocks):
+        sums = sums + state[0, b]
+    total[...] = sums
+    s_tot[...] = sums.astype(BF16)
+    tot_copy = send(s_tot, r_tot, other_core)
+    project(wq, qs, 0, feature_map)
+    relay_y(1)
+    relay_x(0)
+    tot_copy.wait_recv()
+    pair[...] = total[...] + r_tot[...].astype(F32)
+    s_pair[...] = pair[here, :].astype(BF16)
+    pair_copy = send(s_pair, r_pair, other_x)
+    project(wg, gs, 0, silu_by(gain))
+    relay_y(2)
+    relay_x(1)
+    pair_copy.wait_recv()
+    s_grp[...] = (pair[here, :] + r_pair[...].astype(F32)).astype(BF16)
+    grp_copies = [send(s_grp, r_grp.at[d], device) for d, device in enumerate(zs)]
+    ready(0)
+    project(wx.at[0], ks, 1, feature_map)
+    for copy in grp_copies:
+        copy.wait_recv()
+    sums = r_pair[...].astype(F32) * x.astype(F32)
+    for d in range(1, n_z):
+        earlier = jnp.where(z >= d, 1.0, 0.0)
+        sums = sums + r_grp[d - 1].astype(F32) * earlier
+    before[...] = sums
+    s_bef[...] = sums.astype(BF16)
+    bef_copy = send(s_bef, r_bef, other_core)
+    relay_y(3)
+    relay_x(2)
+    ready(1)
+    project(wx.at[1], vs, 1, same)
+    states(1)
+    bef_copy.wait_recv()
+    incoming[here, :] = before[...]
+    incoming[there, :] = r_bef[...].astype(F32)
+    incoming[...] = incoming[...] + r_tot[...].astype(F32) * c.astype(F32)
+    s_inc[...] = incoming[...].astype(BF16)
+    inc_copy = send(s_inc, r_inc, other_y)
+    relay_y(4)
+    relay_x(3)
+    carry(0, incoming)
+    attend(0)
+    relay_x(4)
+    ready(2)
+    project(wx.at[2], qs, 1, feature_map)
+    gain_copy.wait_recv()
+    ready(3)
+    project(wx.at[3], gs, 1, silu_by(gainx))
+    inc_copy.wait_recv()
+    carry(1, r_inc)
+    attend(1)
+    ready(4)
+
+    def project_out(i, _):
+        at = pl.ds(pl.multiple_of(i * BLOCK, BLOCK), BLOCK)
+        w_here = wo[:, pl.ds(pl.multiple_of(h * half, half), half)]
+        first = jnp.dot(qs[0, at, :], w_here, preferred_element_type=F32)
+        second = jnp.dot(qs[1, at, :], wox[...], preferred_element_type=F32)
+        out[at, :] = (first + second).astype(BF16)
+        return 0
+
+    lax.fori_loop(0, blocks, project_out, 0)
+    for copy in copies:
+        copy.wait_send()
+
+
+def on_device_fused(n_tm, frames, conv_weight, w_query, w_key, w_value, w_gate, w_out, norm_gain):
+    rows, depth = frames.shape
+    half = w_query.shape[1]
+    blocks = rows // BLOCK
+    chunk = BLOCK // 2
+    state_rows = half
+    vmem = pl.BlockSpec(memory_space=pltpu.VMEM)
+    act = pltpu.VMEM((2, rows, half), BF16)
+    whole = (state_rows, HEAD_DIM)
+    split = (state_rows // 2, HEAD_DIM)
+    return pl.pallas_call(
+        functools.partial(fused_kernel, n_tm),
+        out_shape=jax.ShapeDtypeStruct((rows, half), BF16),
+        in_specs=[vmem] * 8,
+        out_specs=vmem,
+        scratch_shapes=[
+            pltpu.VMEM((rows, depth), BF16),
+            act, act, act, act,
+            pltpu.VMEM((4, depth, half), BF16),
+            pltpu.VMEM((half, half), BF16),
+            pltpu.VMEM((1, half), F32),
+            pltpu.VMEM((16, depth), BF16),
+            pltpu.VMEM((16 + chunk, depth), F32),
+            pltpu.VMEM((2, blocks) + whole, F32),
+            pltpu.VMEM((2, blocks) + whole, BF16),
+            pltpu.VMEM(whole, F32),
+            pltpu.VMEM(whole, F32),
+            pltpu.VMEM(split, F32),
+            pltpu.VMEM(whole, F32),
+            pltpu.VMEM(whole, BF16), pltpu.VMEM(whole, BF16),
+            pltpu.VMEM(split, BF16), pltpu.VMEM(split, BF16),
+            pltpu.VMEM(split, BF16), pltpu.VMEM((n_tm // 4 - 1,) + split, BF16),
+            pltpu.VMEM(split, BF16), pltpu.VMEM(split, BF16),
+            pltpu.VMEM(whole, BF16), pltpu.VMEM(whole, BF16),
+            pltpu.SemaphoreType.DMA((N_COPIES,)),
+            pltpu.SemaphoreType.DMA((N_COPIES,)),
+        ],
+        compiler_params=pltpu.CompilerParams(
+            collective_id=0, has_side_effects=True, vmem_limit_bytes=60 * 2**20
+        ),
+    )(frames, conv_weight, w_query, w_key, w_value, w_gate, w_out, norm_gain.reshape(1, half))
+
+
 def solution(mesh):
     placed = (
         P("tm", None),
@@ -87,6 +385,11 @@
         P("head", None),
         P("head"),
     )
+    n_tm = mesh.shape["tm"]
+    if mesh.shape["head"] == 2 and n_tm == 16:
+        on_device = functools.partial(on_device_fused, n_tm)
+    else:
+        on_device = on_device_collectives
     return jax.shard_map(
         on_device, mesh=mesh, in_specs=placed, out_specs=P("tm", "head"), check_vma=False
     )

time: 190 us -> 80.8 us (0.43)
  waiting for transfers between devices: 85.9 us -> 0 us
  Pallas kernels: 0 us -> 77.6 us
  matrix products: 44.4 us -> 0 us
  local copies, waits for them, and re-layouts: 27 us -> 3.05 us
  other arithmetic: 15.8 us -> 0 us
  between operations: 13.5 us -> 0.01 us
  starting transfers between devices: 2.39 us -> 0 us
    pallas_call x0 -> x1, Pallas kernels: none -> 77.6 us  [on_device_fused(): pl.pallas_call(functools.partial(fused_kernel, n_tm), out_shape=jax.Shape...]
    reduce_scatter x1 -> x0, waiting for transfers between devices: 53 us -> none  [on_device(): lax.psum_scatter(partial_value.astype(jnp.bfloat16), 'head', scatter_dime...]
    dot_general x7 -> x0, matrix products: 44.4 us -> none  [the longest x1 10.3 us: on_device(): partial_value = jnp.dot(gated, w_out, preferred_element_type=jnp.float32)]
    all_gather x1 -> x0, waiting for transfers between devices: 32.9 us -> none  [on_device(): shard_piece = lax.all_gather(own_total[None], 'tm', axis=0, tiled=True)]
    reshape x4 -> x0, local copies, waits for them, and re-layouts: 13 us -> none  [the longest x2 4.99 us: on_device(): key_blocks = key_feats.reshape(block_shape)]
    convert_element_type x2 -> x0, other arithmetic: 11.6 us -> none  [the longest x1 11.6 us: on_device(): smooth = mixed.astype(jnp.bfloat16)]
    add x1 -> x0, local copies, waits for them, and re-layouts: 5.24 us -> none  [on_device(): attended + jnp.einsum('bthd,bhde->bthe', query_blocks, carried, preferred...]
    mul x1 -> x0, local copies, waits for them, and re-layouts: 3.84 us -> none  [on_device(): attended * lax.rsqrt(mean_square + 1e-06)]
  transfers between devices with their start and end apart: 3 -> 0, of which waited for: 2 -> 0; matrix products, arithmetic and copies ran while one was open for 12% -> 0% of each run, Pallas kernels for 0% -> 0%
where the time goes in v1:
time: 80.8 us; the launch traced here: 80.7 us
  Pallas kernels  77.6 us (96%)
  local copies, waits for them, and re-layouts  3.05 us (4%)
    pallas_call x1, Pallas kernels, on_device_fused(): pl.pallas_call(functools.partial(fused_kernel, n_tm), out_shape=jax.Shape...  77.6 us
    unnamed x1, local copies, waits for them, and re-layouts  3.05 us

profile of v1, /device:TPU:0, one launch (start us, length us, event | category | flops | bytes accessed | tf_op | source)
XLA Modules:
  0.0 80.7 jit_solution(17836284963877190286)
XLA Ops:
  0.0 77.6 %shard_map.82 = bf16[2048,512]{1,0:T(8,128)(2,1)} custom-call(bf16[2048,1024]{1,0:T(8,128)(2,1)} %frames.1, bf16[4,1024]{1,0:T(4,128)(2,1)} %conv.1, bf16[1024,512]{1,0:T(8,128)(2,1)} %wq.1, bf16[1024,512]{1,0:T(8,128)(2,1)} %wk.1, bf16[1024,512]{1,0:T(8,128)(2,1)} %wv.1, bf16[1024,512]{1,0:T(8,128)(2,1)} %wg.1, bf16[512,1024]{1,0:T(8,128)(2,1)} %wo.1, ...), custom_call_target="tpu_custom_call" | custom-call | tf_op jit(solution)/shard_map/pallas_call | solution.py:344
  77.6 3.0 %copy.10 = bf16[2048,512]{1,0:T(8,128)(2,1)} copy(bf16[2048,512]{1,0:T(8,128)(2,1)} %shard_map.82) | data formatting | bytes 4194304

commit v2 on v1

--- a/solution.py
+++ b/solution.py
@@ -87,11 +87,12 @@
 
 
 def fused_kernel(
-    n_tm, frames, conv, wq, wk, wv, wg, wo, gain, out,
-    smooth, qs, ks, vs, gs, wx, wox, gainx, halo, ext, state, carried,
+    n_tm, frames_hbm, conv, wq, wk, wv, wg, wo, gain, out_hbm,
+    frames, own, wo_own, out,
+    smooth, qs, ks, vs, gs, wx, wox, gainx, halo, ext_a, ext_b, state, carried,
     total, pair, before, incoming,
     s_tot, r_tot, s_pair, r_pair, s_grp, r_grp, s_bef, r_bef, s_inc, r_inc,
-    send_sem, recv_sem,
+    send_sem, recv_sem, load_sem, store_sem,
 ):
     t = lax.axis_index("tm")
     h = lax.axis_index("head")
@@ -115,6 +116,20 @@
     zs = [{"tm": lax.rem(z + d, n_z) * 4 + r} for d in range(1, n_z)]
     r_x = r + 2 - 4 * x
 
+    loads = {}
+
+    def load(name, src, dst):
+        n = len(loads)
+        loads[name] = pltpu.make_async_copy(src, dst, load_sem.at[n])
+        loads[name].start()
+
+    for b in range(blocks):
+        at = pl.ds(b * BLOCK, BLOCK)
+        load(b, frames_hbm.at[at, :], frames.at[at, :])
+    for m, weight in enumerate((wk, wv, wq, wg)):
+        load(("own", m), weight, own.at[m])
+    load("out", wo.at[:, pl.ds(pl.multiple_of(h * half, half), half)], wo_own)
+
     barrier = pltpu.get_barrier_semaphore()
     peers = [other_core, other_x, other_y, after, ahead] + zs
     for peer in peers:
@@ -138,7 +153,7 @@
             return wox.at[pl.ds(pl.multiple_of(which * quarter_o, quarter_o), quarter_o), :]
         return wx.at[m, pl.ds(pl.multiple_of(which * quarter, quarter), quarter), :]
 
-    edge = send(frames.at[pl.ds(rows - 16, 16), :], halo, after)
+    edge = send(frames_hbm.at[pl.ds(rows - 16, 16), :], halo, after)
     from_y, from_x, from_core = {}, {}, {}
     for m, weight in enumerate((wk, wv, wq, wg)):
         mine = weight.at[pl.ds(pl.multiple_of(r * quarter, quarter), quarter), :]
@@ -166,51 +181,61 @@
     chunk = BLOCK // 2
     taps = conv[...].astype(F32)
 
-    def mix(first):
-        ext[16 : 16 + chunk, :] = frames[pl.ds(first, chunk), :].astype(F32)
-        mixed = taps[0:1] * ext[13 : 13 + chunk, :]
-        for j in range(1, CONV):
-            mixed = mixed + taps[j : j + 1] * ext[13 + j : 13 + j + chunk, :]
-        smooth[pl.ds(first, chunk), :] = mixed.astype(BF16)
-
-    def mix_chunk(i, _):
-        first = pl.multiple_of(i * chunk, chunk)
-        ext[0:16, :] = frames[pl.ds(pl.multiple_of(first - 16, 16), 16), :].astype(F32)
-        mix(first)
-        return 0
-
-    lax.fori_loop(1, rows // chunk, mix_chunk, 0)
-    edge.wait_recv()
-    ext[0:16, :] = halo[...].astype(F32) * jnp.minimum(t, 1).astype(F32)
-    mix(0)
-
-    def project(weight, into, which, function):
+    def mix(b):
+        for part, ext in ((0, ext_a), (1, ext_b)):
+            first = b * BLOCK + part * chunk
+            if first == 0:
+                ext[0:16, :] = halo[...].astype(F32) * jnp.minimum(t, 1).astype(F32)
+            else:
+                ext[0:16, :] = frames[first - 16 : first, :].astype(F32)
+            ext[16 : 16 + chunk, :] = frames[first : first + chunk, :].astype(F32)
+            mixed = taps[0:1] * ext[13 : 13 + chunk, :]
+            for j in range(1, CONV):
+                mixed = mixed + taps[j : j + 1] * ext[13 + j : 13 + j + chunk, :]
+            smooth[first : first + chunk, :] = mixed.astype(BF16)
+
+    wide = 2 * HEAD_DIM
+
+    def project_block(at, jobs):
+        for weight, into, which, function in jobs:
+            for first in range(0, half, wide):
+                cols = slice(first, first + wide)
+                product = jnp.dot(smooth[at, :], weight[:, cols], preferred_element_type=F32)
+                into[which, at, cols] = function(product, cols).astype(BF16)
+
+    def project(jobs):
         def step(i, _):
-            at = pl.ds(pl.multiple_of(i * BLOCK, BLOCK), BLOCK)
-            product = jnp.dot(smooth[at, :], weight[...], preferred_element_type=F32)
-            into[which, at, :] = function(product).astype(BF16)
+            for u in range(2):
+                project_block(pl.ds(pl.multiple_of((2 * i + u) * BLOCK, BLOCK), BLOCK), jobs)
             return 0
 
-        lax.fori_loop(0, blocks, step, 0)
+        lax.fori_loop(0, blocks // 2, step, 0)
+
+    def features(v, cols):
+        return feature_map(v)
 
     def silu_by(gain_ref):
-        def function(v):
-            return (0.5 * v) * (1.0 + jnp.tanh(0.5 * v)) * gain_ref[...]
+        def function(v, cols):
+            return (0.5 * v) * (1.0 + jnp.tanh(0.5 * v)) * gain_ref[:, cols]
 
         return function
 
-    def same(v):
+    def same(v, cols):
         return v
 
     def states(which):
         def step(b, _):
             at = pl.ds(pl.multiple_of(b * BLOCK, BLOCK), BLOCK)
-            for j in range(heads):
-                cols = slice(j * HEAD_DIM, (j + 1) * HEAD_DIM)
-                state[which, b, cols, :] = lax.dot_general(
+            for first in range(0, half, wide):
+                cols = slice(first, first + wide)
+                both = lax.dot_general(
                     ks[which, at, cols], vs[which, at, cols],
                     (((0,), (0,)), ((), ())), preferred_element_type=F32,
                 )
+                for j in range(0, wide, HEAD_DIM):
+                    state[which, b, first + j : first + j + HEAD_DIM, :] = both[
+                        j : j + HEAD_DIM, j : j + HEAD_DIM
+                    ]
             return 0
 
         lax.fori_loop(0, blocks, step, 0)
@@ -242,11 +267,14 @@
                 s11 = lax.dot_general(q1, k1, nt, preferred_element_type=F32)
                 s00 = jnp.where(causal, s00, 0.0).astype(BF16)
                 s11 = jnp.where(causal, s11, 0.0).astype(BF16)
-                a0 = jnp.dot(s00, v0, preferred_element_type=F32)
-                a0 = a0 + jnp.dot(q0, start, preferred_element_type=F32)
-                a1 = jnp.dot(s10.astype(BF16), v0, preferred_element_type=F32)
-                a1 = a1 + jnp.dot(s11, v1, preferred_element_type=F32)
-                a1 = a1 + jnp.dot(q1, start, preferred_element_type=F32)
+                a0 = jnp.dot(
+                    jnp.concatenate([s00, q0], axis=1),
+                    jnp.concatenate([v0, start], axis=0), preferred_element_type=F32,
+                )
+                a1 = jnp.dot(
+                    jnp.concatenate([s10.astype(BF16), s11, q1], axis=1),
+                    jnp.concatenate([v0, v1, start], axis=0), preferred_element_type=F32,
+                )
                 for at, a in ((low, a0), (high, a1)):
                     scale = lax.rsqrt(jnp.mean(a * a, axis=-1, keepdims=True) + 1e-06)
                     gated = a * scale * gs[which, at, cols].astype(F32)
@@ -258,9 +286,25 @@
     here = pl.ds(pl.multiple_of(c * (half // 2), half // 2), half // 2)
     there = pl.ds(pl.multiple_of((1 - c) * (half // 2), half // 2), half // 2)
 
-    project(wk, ks, 0, feature_map)
+    own_kv = [(own.at[0], ks, 0, features), (own.at[1], vs, 0, same)]
+
+    def first_block(b):
+        project_block(pl.ds(b * BLOCK, BLOCK), own_kv)
+
+    loads[0].wait()
+    for b in range(1, blocks):
+        loads[b].wait()
+        if b == 2:
+            loads["own", 0].wait()
+            loads["own", 1].wait()
+        mix(b)
+        if b > 1:
+            first_block(b - 1)
+    edge.wait_recv()
     relay_y(0)
-    project(wv, vs, 0, same)
+    mix(0)
+    first_block(blocks - 1)
+    first_block(0)
     states(0)
     sums = state[0, 0]
     for b in range(1, blocks):
@@ -268,21 +312,23 @@
     total[...] = sums
     s_tot[...] = sums.astype(BF16)
     tot_copy = send(s_tot, r_tot, other_core)
-    project(wq, qs, 0, feature_map)
     relay_y(1)
     relay_x(0)
+    loads["own", 2].wait()
+    project([(own.at[2], qs, 0, features)])
     tot_copy.wait_recv()
     pair[...] = total[...] + r_tot[...].astype(F32)
     s_pair[...] = pair[here, :].astype(BF16)
     pair_copy = send(s_pair, r_pair, other_x)
-    project(wg, gs, 0, silu_by(gain))
+    loads["own", 3].wait()
+    project([(own.at[3], gs, 0, silu_by(gain))])
     relay_y(2)
     relay_x(1)
     pair_copy.wait_recv()
     s_grp[...] = (pair[here, :] + r_pair[...].astype(F32)).astype(BF16)
     grp_copies = [send(s_grp, r_grp.at[d], device) for d, device in enumerate(zs)]
     ready(0)
-    project(wx.at[0], ks, 1, feature_map)
+    project([(wx.at[0], ks, 1, features)])
     for copy in grp_copies:
         copy.wait_recv()
     sums = r_pair[...].astype(F32) * x.astype(F32)
@@ -295,7 +341,7 @@
     relay_y(3)
     relay_x(2)
     ready(1)
-    project(wx.at[1], vs, 1, same)
+    project([(wx.at[1], vs, 1, same)])
     states(1)
     bef_copy.wait_recv()
     incoming[here, :] = before[...]
@@ -309,24 +355,28 @@
     attend(0)
     relay_x(4)
     ready(2)
-    project(wx.at[2], qs, 1, feature_map)
+    ready(3)
     gain_copy.wait_recv()
-    ready(3)
-    project(wx.at[3], gs, 1, silu_by(gainx))
+    project([(wx.at[2], qs, 1, features), (wx.at[3], gs, 1, silu_by(gainx))])
     inc_copy.wait_recv()
     carry(1, r_inc)
     attend(1)
     ready(4)
 
-    def project_out(i, _):
-        at = pl.ds(pl.multiple_of(i * BLOCK, BLOCK), BLOCK)
-        w_here = wo[:, pl.ds(pl.multiple_of(h * half, half), half)]
-        first = jnp.dot(qs[0, at, :], w_here, preferred_element_type=F32)
-        second = jnp.dot(qs[1, at, :], wox[...], preferred_element_type=F32)
-        out[at, :] = (first + second).astype(BF16)
-        return 0
-
-    lax.fori_loop(0, blocks, project_out, 0)
+    loads["out"].wait()
+    stores = []
+    for b in range(blocks):
+        at = pl.ds(b * BLOCK, BLOCK)
+        for first in range(0, half, wide):
+            cols = slice(first, first + wide)
+            here_part = jnp.dot(qs[0, at, :], wo_own[:, cols], preferred_element_type=F32)
+            there_part = jnp.dot(qs[1, at, :], wox[:, cols], preferred_element_type=F32)
+            out[at, cols] = (here_part + there_part).astype(BF16)
+        store = pltpu.make_async_copy(out.at[at, :], out_hbm.at[at, :], store_sem.at[b])
+        store.start()
+        stores.append(store)
+    for store in stores:
+        store.wait()
     for copy in copies:
         copy.wait_send()
 
@@ -338,21 +388,27 @@
     chunk = BLOCK // 2
     state_rows = half
     vmem = pl.BlockSpec(memory_space=pltpu.VMEM)
+    hbm = pl.BlockSpec(memory_space=pl.ANY)
     act = pltpu.VMEM((2, rows, half), BF16)
     whole = (state_rows, HEAD_DIM)
     split = (state_rows // 2, HEAD_DIM)
     return pl.pallas_call(
         functools.partial(fused_kernel, n_tm),
         out_shape=jax.ShapeDtypeStruct((rows, half), BF16),
-        in_specs=[vmem] * 8,
-        out_specs=vmem,
+        in_specs=[hbm, vmem] + [hbm] * 5 + [vmem],
+        out_specs=hbm,
         scratch_shapes=[
+            pltpu.VMEM((rows, depth), BF16),
+            pltpu.VMEM((4, depth, half), BF16),
+            pltpu.VMEM((half, half), BF16),
+            pltpu.VMEM((rows, half), BF16),
             pltpu.VMEM((rows, depth), BF16),
             act, act, act, act,
             pltpu.VMEM((4, depth, half), BF16),
             pltpu.VMEM((half, half), BF16),
             pltpu.VMEM((1, half), F32),
             pltpu.VMEM((16, depth), BF16),
+            pltpu.VMEM((16 + chunk, depth), F32),
             pltpu.VMEM((16 + chunk, depth), F32),
             pltpu.VMEM((2, blocks) + whole, F32),
             pltpu.VMEM((2, blocks) + whole, BF16),
@@ -367,6 +423,8 @@
             pltpu.VMEM(whole, BF16), pltpu.VMEM(whole, BF16),
             pltpu.SemaphoreType.DMA((N_COPIES,)),
             pltpu.SemaphoreType.DMA((N_COPIES,)),
+            pltpu.SemaphoreType.DMA((blocks + 5,)),
+            pltpu.SemaphoreType.DMA((blocks,)),
         ],
         compiler_params=pltpu.CompilerParams(
             collective_id=0, has_side_effects=True, vmem_limit_bytes=60 * 2**20

time: 80.8 us -> 71.9 us (0.89)
  Pallas kernels: 77.6 us -> 68.6 us
    pallas_call x1, Pallas kernels: 77.6 us -> 68.6 us  [on_device_fused(): pl.pallas_call(functools.partial(fused_kernel, n_tm), out_shape=jax.Shape...]
where the time goes in v2:
time: 71.9 us; the launch traced here: 71.7 us
  Pallas kernels  68.6 us (95%)
  local copies, waits for them, and re-layouts  3.05 us (4%)
    pallas_call x1, Pallas kernels, on_device_fused(): pl.pallas_call(functools.partial(fused_kernel, n_tm), out_shape=jax.Shape...  68.6 us
    unnamed x1, local copies, waits for them, and re-layouts  3.05 us

profile of v2, /device:TPU:0, one launch (start us, length us, event | category | flops | bytes accessed | tf_op | source)
XLA Modules:
  0.0 71.7 jit_solution(9518235391988990727)
XLA Ops:
  0.0 68.6 %shard_map.82 = bf16[2048,512]{1,0:T(8,128)(2,1)} custom-call(bf16[2048,1024]{1,0:T(8,128)(2,1)} %frames_hbm.1, bf16[4,1024]{1,0:T(4,128)(2,1)} %conv.1, bf16[1024,512]{1,0:T(8,128)(2,1)} %wq.1, bf16[1024,512]{1,0:T(8,128)(2,1)} %wk.1, bf16[1024,512]{1,0:T(8,128)(2,1)} %wv.1, bf16[1024,512]{1,0:T(8,128)(2,1)} %wg.1, bf16[512,1024]{1,0:T(8,128)(2,1)} %wo.1, ...), custom_call_target="tpu_custom_call" | custom-call | tf_op jit(solution)/shard_map/pallas_call | solution.py:395
  68.6 3.0 %copy.10 = bf16[2048,512]{1,0:T(8,128)(2,1)} copy(bf16[2048,512]{1,0:T(8,128)(2,1)} %shard_map.82) | data formatting | bytes 4194304

commit v3 on v2

--- a/solution.py
+++ b/solution.py
@@ -155,14 +155,19 @@
 
     edge = send(frames_hbm.at[pl.ds(rows - 16, 16), :], halo, after)
     from_y, from_x, from_core = {}, {}, {}
-    for m, weight in enumerate((wk, wv, wq, wg)):
-        mine = weight.at[pl.ds(pl.multiple_of(r * quarter, quarter), quarter), :]
+
+    def start_y(m):
+        if m < 4:
+            weight = (wk, wv, wq, wg)[m]
+            mine = weight.at[pl.ds(pl.multiple_of(r * quarter, quarter), quarter), :]
+        else:
+            mine = wo.at[
+                pl.ds(pl.multiple_of(r * quarter_o, quarter_o), quarter_o),
+                pl.ds(pl.multiple_of((1 - h) * half, half), half),
+            ]
         from_y[m] = send(mine, piece(m, r), other_y)
-    mine = wo.at[
-        pl.ds(pl.multiple_of(r * quarter_o, quarter_o), quarter_o),
-        pl.ds(pl.multiple_of((1 - h) * half, half), half),
-    ]
-    from_y[4] = send(mine, piece(4, r), other_y)
+
+    start_y(0)
     gain_copy = send(gain, gainx, other_y)
 
     def relay_y(m):
@@ -252,7 +257,7 @@
     causal = col_id <= row_id
     nt = (((1,), (1,)), ((), ()))
 
-    def attend(which):
+    def attend(which, lower, upper):
         def step(b, _):
             low = pl.ds(pl.multiple_of(b * BLOCK, BLOCK), chunk)
             high = pl.ds(pl.multiple_of(b * BLOCK + chunk, chunk), chunk)
@@ -281,7 +286,7 @@
                     qs[which, at, cols] = gated.astype(BF16)
             return 0
 
-        lax.fori_loop(0, blocks, step, 0)
+        lax.fori_loop(lower, upper, step, 0)
 
     here = pl.ds(pl.multiple_of(c * (half // 2), half // 2), half // 2)
     there = pl.ds(pl.multiple_of((1 - c) * (half // 2), half // 2), half // 2)
@@ -300,11 +305,13 @@
         mix(b)
         if b > 1:
             first_block(b - 1)
+        if b in (1, 3):
+            start_y((b + 1) // 2)
     edge.wait_recv()
-    relay_y(0)
     mix(0)
     first_block(blocks - 1)
     first_block(0)
+    relay_y(0)
     states(0)
     sums = state[0, 0]
     for b in range(1, blocks):
@@ -312,21 +319,21 @@
     total[...] = sums
     s_tot[...] = sums.astype(BF16)
     tot_copy = send(s_tot, r_tot, other_core)
-    relay_y(1)
-    relay_x(0)
     loads["own", 2].wait()
     project([(own.at[2], qs, 0, features)])
+    start_y(3)
     tot_copy.wait_recv()
     pair[...] = total[...] + r_tot[...].astype(F32)
     s_pair[...] = pair[here, :].astype(BF16)
     pair_copy = send(s_pair, r_pair, other_x)
+    relay_y(1)
     loads["own", 3].wait()
     project([(own.at[3], gs, 0, silu_by(gain))])
-    relay_y(2)
-    relay_x(1)
+    start_y(4)
     pair_copy.wait_recv()
     s_grp[...] = (pair[here, :] + r_pair[...].astype(F32)).astype(BF16)
     grp_copies = [send(s_grp, r_grp.at[d], device) for d, device in enumerate(zs)]
+    relay_x(0)
     ready(0)
     project([(wx.at[0], ks, 1, features)])
     for copy in grp_copies:
@@ -338,8 +345,8 @@
     before[...] = sums
     s_bef[...] = sums.astype(BF16)
     bef_copy = send(s_bef, r_bef, other_core)
-    relay_y(3)
-    relay_x(2)
+    relay_y(2)
+    relay_x(1)
     ready(1)
     project([(wx.at[1], vs, 1, same)])
     states(1)
@@ -349,18 +356,22 @@
     incoming[...] = incoming[...] + r_tot[...].astype(F32) * c.astype(F32)
     s_inc[...] = incoming[...].astype(BF16)
     inc_copy = send(s_inc, r_inc, other_y)
+    carry(0, incoming)
+    attend(0, 0, blocks // 2)
+    relay_y(3)
+    relay_x(2)
+    attend(0, blocks // 2, blocks)
     relay_y(4)
+    ready(2)
+    project([(wx.at[2], qs, 1, features)])
     relay_x(3)
-    carry(0, incoming)
-    attend(0)
-    relay_x(4)
-    ready(2)
     ready(3)
     gain_copy.wait_recv()
-    project([(wx.at[2], qs, 1, features), (wx.at[3], gs, 1, silu_by(gainx))])
+    project([(wx.at[3], gs, 1, silu_by(gainx))])
+    relay_x(4)
     inc_copy.wait_recv()
     carry(1, r_inc)
-    attend(1)
+    attend(1, 0, blocks)
     ready(4)
 
     loads["out"].wait()

time: 71.9 us -> 70.8 us (0.985)
  Pallas kernels: 68.6 us -> 67.5 us
    pallas_call x1, Pallas kernels: 68.6 us -> 67.5 us  [on_device_fused(): pl.pallas_call(functools.partial(fused_kernel, n_tm), out_shape=jax.Shape...]
where the time goes in v3:
time: 70.8 us; the launch traced here: 70.6 us
  Pallas kernels  67.5 us (95%)
  local copies, waits for them, and re-layouts  3.05 us (4%)
    pallas_call x1, Pallas kernels, on_device_fused(): pl.pallas_call(functools.partial(fused_kernel, n_tm), out_shape=jax.Shape...  67.5 us
    unnamed x1, local copies, waits for them, and re-layouts  3.05 us

profile of v3, /device:TPU:0, one launch (start us, length us, event | category | flops | bytes accessed | tf_op | source)
XLA Modules:
  0.0 70.6 jit_solution(12223091387919665192)
XLA Ops:
  0.0 67.5 %shard_map.82 = bf16[2048,512]{1,0:T(8,128)(2,1)} custom-call(bf16[2048,1024]{1,0:T(8,128)(2,1)} %frames_hbm.1, bf16[4,1024]{1,0:T(4,128)(2,1)} %conv.1, bf16[1024,512]{1,0:T(8,128)(2,1)} %wq.1, bf16[1024,512]{1,0:T(8,128)(2,1)} %wk.1, bf16[1024,512]{1,0:T(8,128)(2,1)} %wv.1, bf16[1024,512]{1,0:T(8,128)(2,1)} %wg.1, bf16[512,1024]{1,0:T(8,128)(2,1)} %wo.1, ...), custom_call_target="tpu_custom_call" | custom-call | tf_op jit(solution)/shard_map/pallas_call | solution.py:406
  67.5 3.0 %copy.10 = bf16[2048,512]{1,0:T(8,128)(2,1)} copy(bf16[2048,512]{1,0:T(8,128)(2,1)} %shard_map.82) | data formatting | bytes 4194304

commit v4 on v3

--- a/solution.py
+++ b/solution.py
@@ -209,12 +209,8 @@
                 into[which, at, cols] = function(product, cols).astype(BF16)
 
     def project(jobs):
-        def step(i, _):
-            for u in range(2):
-                project_block(pl.ds(pl.multiple_of((2 * i + u) * BLOCK, BLOCK), BLOCK), jobs)
-            return 0
-
-        lax.fori_loop(0, blocks // 2, step, 0)
+        for b in range(blocks):
+            project_block(pl.ds(b * BLOCK, BLOCK), jobs)
 
     def features(v, cols):
         return feature_map(v)
@@ -258,7 +254,7 @@
     nt = (((1,), (1,)), ((), ()))
 
     def attend(which, lower, upper):
-        def step(b, _):
+        def one(b):
             low = pl.ds(pl.multiple_of(b * BLOCK, BLOCK), chunk)
             high = pl.ds(pl.multiple_of(b * BLOCK + chunk, chunk), chunk)
             for j in range(heads):
@@ -284,9 +280,12 @@
                     scale = lax.rsqrt(jnp.mean(a * a, axis=-1, keepdims=True) + 1e-06)
                     gated = a * scale * gs[which, at, cols].astype(F32)
                     qs[which, at, cols] = gated.astype(BF16)
+        def step(i, _):
+            one(2 * i)
+            one(2 * i + 1)
             return 0
 
-        lax.fori_loop(lower, upper, step, 0)
+        lax.fori_loop(lower // 2, upper // 2, step, 0)
 
     here = pl.ds(pl.multiple_of(c * (half // 2), half // 2), half // 2)
     there = pl.ds(pl.multiple_of((1 - c) * (half // 2), half // 2), half // 2)

time: 70.8 us -> 68.8 us (0.972)
  Pallas kernels: 67.5 us -> 65.6 us
    pallas_call x1, Pallas kernels: 67.5 us -> 65.6 us  [on_device_fused(): pl.pallas_call(functools.partial(fused_kernel, n_tm), out_shape=jax.Shape...]
where the time goes in v4:
time: 68.8 us; the launch traced here: 68.6 us
  Pallas kernels  65.6 us (95%)
  local copies, waits for them, and re-layouts  3.05 us (4%)
    pallas_call x1, Pallas kernels, on_device_fused(): pl.pallas_call(functools.partial(fused_kernel, n_tm), out_shape=jax.Shape...  65.6 us
    unnamed x1, local copies, waits for them, and re-layouts  3.05 us

profile of v4, /device:TPU:0, one launch (start us, length us, event | category | flops | bytes accessed | tf_op | source)
XLA Modules:
  0.0 68.6 jit_solution(14491521583203102561)
XLA Ops:
  0.0 65.6 %shard_map.82 = bf16[2048,512]{1,0:T(8,128)(2,1)} custom-call(bf16[2048,1024]{1,0:T(8,128)(2,1)} %frames_hbm.1, bf16[4,1024]{1,0:T(4,128)(2,1)} %conv.1, bf16[1024,512]{1,0:T(8,128)(2,1)} %wq.1, bf16[1024,512]{1,0:T(8,128)(2,1)} %wk.1, bf16[1024,512]{1,0:T(8,128)(2,1)} %wv.1, bf16[1024,512]{1,0:T(8,128)(2,1)} %wg.1, bf16[512,1024]{1,0:T(8,128)(2,1)} %wo.1, ...), custom_call_target="tpu_custom_call" | custom-call | tf_op jit(solution)/shard_map/pallas_call | solution.py:405
  65.6 3.0 %copy.10 = bf16[2048,512]{1,0:T(8,128)(2,1)} copy(bf16[2048,512]{1,0:T(8,128)(2,1)} %shard_map.82) | data formatting | bytes 4194304
